TPU v7x, 256 devices: a whole 4x4x8 slice. The times are simulated.
256 devices in a mesh: dp: 32 (over x, y, core), expert: 8 (over z).
Axes of the slice: x: 4, y: 4, z: 8, core: 2. Of those that a mesh axis runs over, the one named last changes fastest.
Arguments:
- tokens: bfloat16 [32768, 4096], P(('dp', 'expert')), may hold values from -6 to 6
- router_weight: float32 [4096, 128], replicated, may hold values from -0.1875 to 0.1875
- rollout_ids: int32 [32768, 8], P(('dp', 'expert')), may hold values from 0 to 127, all different within a row; in each aligned block of 128 rows (0 to 127, 128 to 255, ...) at most 9 rows name the same one
- source_row: int32 [32768], P(('dp', 'expert')), may hold values from 0 to 32767, as said below
- gate_weight: bfloat16 [32, 4096, 1536], P('dp', None, 'expert'), may hold values from -0.09375 to 0.09375
- up_weight: bfloat16 [32, 4096, 1536], P('dp', None, 'expert'), may hold values from -0.09375 to 0.09375
- down_weight: bfloat16 [32, 1536, 4096], P('dp', None, 'expert'), may hold values from -0.15625 to 0.15625
Outputs:
- layer_out: bfloat16 [32768, 4096], P(('dp', 'expert'))
Inputs may be any that keep to these rules, and one draw needn't show every extreme that they name: `rollout_ids`: each row names 8 different experts. In every aligned block of 128 rows no expert is named by more than 9 rows, a bound that some block reaches. `source_row`: A permutation of the 32768 rows. The 128 trainer rows of an aligned block all read rows of one aligned block of 128 rollout rows, the blocks correspond one to one, and a trainer block's index and its rollout block's index are equal modulo 8.
All inputs are finite; a program needn't handle non-finite values.
Results may differ from a plain program's by a relative error of at most 0.0058.
Values may be sent and summed in bfloat16 or wider, within the bound.
No kernel may reach another device: no remote copies, remote signals or barrier semaphores. Data moves between devices by JAX's collectives and lax.ppermute only.
A program may use at most 128 MiB of HBM per device.

v0:
```python
import functools

import jax
import jax.numpy as jnp
from jax import lax
from jax.experimental import pallas as pl
from jax.experimental.pallas import tpu as pltpu
from jax.sharding import PartitionSpec as P

MAIN = 8
FIRST_WIDTH = 1536
HIDDEN_STEPS = 3
CUT = 4
DISPATCH_STEPS = 1
VMEM_BYTES = 48 * 1024 * 1024
bf16, f32 = jnp.bfloat16, jnp.float32


def iota(shape, dim):
    return lax.broadcasted_iota(jnp.int32, shape, dim)


def first_dispatch_kernel(columns, tok_rows, rank_ref, raw_ref, out_ref, pair_sel, last_sel):
    owners = rank_ref.shape[0]
    pairs = columns // 2
    pair_toks, pair_rows = 2 * tok_rows, 2 * MAIN

    @pl.when(pl.program_id(0) == 0)
    def _():
        row, tok = iota((pair_rows, pair_toks), 0), iota((pair_rows, pair_toks), 1)
        wanted = jnp.where(row // MAIN == tok // tok_rows, row % MAIN, -2).astype(f32)
        for pair in range(pairs):
            rank = rank_ref[:, :, pair * pair_toks : (pair + 1) * pair_toks]
            sel = jnp.where(rank == wanted[None], 1.0, 0.0).astype(bf16)
            pair_sel[pair] = sel.reshape(owners * pair_rows, pair_toks)
        row, tok = iota((columns, columns * tok_rows), 0), iota((columns, columns * tok_rows), 1)
        wanted = jnp.where(row == tok // tok_rows, MAIN, -2).astype(f32)
        sel = jnp.where(rank_ref[...] == wanted[None], 1.0, 0.0)
        last_sel[...] = sel.reshape(owners * columns, columns * tok_rows).astype(bf16)

    for pair in range(pairs):
        rows = jnp.dot(
            pair_sel[pair],
            raw_ref[pair * pair_toks : (pair + 1) * pair_toks, :],
            preferred_element_type=f32,
        ).astype(bf16)
        out_ref[:, pair * pair_rows : (pair + 1) * pair_rows, :] = rows.reshape(
            owners, pair_rows, rows.shape[1]
        )
    rows = jnp.dot(last_sel[...], raw_ref[...], preferred_element_type=f32)
    out_ref[:, columns * MAIN :, :] = rows.reshape(owners, columns, rows.shape[1]).astype(bf16)


def first_dispatch(rank, raw, columns, tok_rows):
    owners = rank.shape[0]
    row_toks, width = raw.shape
    block_rows = columns * (MAIN + 1)
    pairs = columns // 2
    return pl.pallas_call(
        functools.partial(first_dispatch_kernel, columns, tok_rows),
        grid=(DISPATCH_STEPS,),
        in_specs=[
            pl.BlockSpec((owners, 1, row_toks), lambda f: (0, 0, 0)),
            pl.BlockSpec((row_toks, width // DISPATCH_STEPS), lambda f: (0, f)),
        ],
        out_specs=pl.BlockSpec((owners, block_rows, width // DISPATCH_STEPS), lambda f: (0, 0, f)),
        out_shape=jax.ShapeDtypeStruct((owners, block_rows, width), bf16),
        scratch_shapes=[
            pltpu.VMEM((pairs, owners * 2 * MAIN, 2 * tok_rows), bf16),
            pltpu.VMEM((owners * columns, row_toks), bf16),
        ],
        compiler_params=pltpu.CompilerParams(vmem_limit_bytes=VMEM_BYTES),
    )(rank, raw)


def hidden_kernel(rows, cut, x_ref, w_ref, v_ref, near_ref, far_ref, last_sum):
    columns, step_rows, width = x_ref.shape
    units = w_ref.shape[1]
    lanes = 128
    sources = rows // MAIN
    hidden_part = near_ref.shape[0]
    acc = jnp.dot(
        x_ref[...].reshape(columns * step_rows, width), w_ref[...], preferred_element_type=f32
    )

    def silu_times(gate, up):
        return gate / (1.0 + jnp.exp(-gate)) * up

    def store(ref, val, at):
        whole = (units // 2) // lanes * lanes
        tail = val[:, 2 * whole :]
        hidden = jnp.concatenate(
            [
                silu_times(val[:, :whole], val[:, whole : 2 * whole]),
                silu_times(tail, pltpu.roll(tail, lanes // 2, 1)),
            ],
            axis=1,
        )
        ref[:, at : at + val.shape[0]] = hidden.T[:hidden_part].astype(bf16)

    def finish(step, blocks, with_last):
        first_source = step * (step_rows // rows) * sources
        for ref, lowest, highest in ((near_ref, 0, cut), (far_ref, cut, columns)):
            count = (highest - lowest) * MAIN
            pieces = [
                acc[(j * step_rows + i) : (j * step_rows + i + MAIN)]
                for i in range(0, blocks * rows, MAIN)
                for j in range(lowest, highest)
            ]
            val = v_ref[first_source : first_source + blocks * sources, lowest * MAIN : highest * MAIN]
            val = val.reshape(blocks * sources * count, units) + jnp.concatenate(pieces, axis=0)
            store(ref, val, first_source * count)
        if with_last:
            for j in range(columns):
                at = j * step_rows + blocks * rows
                last_sum[j] = acc[at : at + rows]
            val = jnp.concatenate([last_sum[:, i, :] for i in range(rows)], axis=0)
            val = val + v_ref[:, columns * MAIN :].reshape(rows * columns, units)
            store(far_ref, val, rows * (columns - cut) * MAIN)

    for step in range(HIDDEN_STEPS):
        blocks = step_rows // rows
        with_last = step == HIDDEN_STEPS - 1
        pl.when(pl.program_id(0) == step)(
            functools.partial(finish, step, blocks - with_last, with_last)
        )


def hidden_rows(gathered, weight, first_val, hidden_part, cut):
    columns, col_rows, width = gathered.shape
    owners, block_rows, units = first_val.shape
    steps = HIDDEN_STEPS
    step_rows = col_rows // steps
    near = owners * cut * MAIN
    far = owners * block_rows - near
    return pl.pallas_call(
        functools.partial(hidden_kernel, owners, cut),
        grid=(steps,),
        in_specs=[
            pl.BlockSpec((columns, step_rows, width), lambda b: (0, b, 0)),
            pl.BlockSpec(weight.shape, lambda b: (0, 0)),
            pl.BlockSpec(first_val.shape, lambda b: (0, 0, 0)),
        ],
        out_specs=[
            pl.BlockSpec((hidden_part, near), lambda b: (0, 0)),
            pl.BlockSpec((hidden_part, far), lambda b: (0, 0)),
        ],
        out_shape=[
            jax.ShapeDtypeStruct((hidden_part, near), bf16),
            jax.ShapeDtypeStruct((hidden_part, far), bf16),
        ],
        scratch_shapes=[pltpu.VMEM((columns, owners, units), f32)],
        compiler_params=pltpu.CompilerParams(vmem_limit_bytes=VMEM_BYTES),
    )(gathered, weight, first_val)


def combine_kernel(columns, pair_high, pair_low, last_high, last_low, back_ref, out_ref):
    owners, block_rows, width = back_ref.shape
    pairs, pair_toks, pair_rows = pair_high.shape
    rows = pair_rows // owners
    last = back_ref[:, columns * MAIN :, :].reshape(owners * columns, width)
    for pair in range(pairs):
        back = back_ref[:, pair * rows : (pair + 1) * rows, :].reshape(pair_rows, width)
        toks = slice(pair * pair_toks, (pair + 1) * pair_toks)
        part = jnp.dot(pair_high[pair], back, preferred_element_type=f32)
        part = part + jnp.dot(pair_low[pair], back, preferred_element_type=f32)
        part = part + jnp.dot(last_high[toks], last, preferred_element_type=f32)
        part = part + jnp.dot(last_low[toks], last, preferred_element_type=f32)
        out_ref[toks] = part.astype(bf16)


def combine(mats, back, columns):
    row_toks = mats[2].shape[0]
    return pl.pallas_call(
        functools.partial(combine_kernel, columns),
        out_shape=jax.ShapeDtypeStruct((row_toks, back.shape[2]), bf16),
        compiler_params=pltpu.CompilerParams(vmem_limit_bytes=VMEM_BYTES),
    )(*mats, back)


def combine_matrices(rank, weight, columns, tok_rows):
    row_toks, owners = rank.shape
    high = lax.reduce_precision(weight, 8, 7)
    parts = [high.astype(bf16), (weight - high).astype(bf16)]
    column = jnp.arange(row_toks, dtype=jnp.int32)[:, None] // tok_rows

    def matrix(count, row_column, row_slot):
        lane = jnp.arange(owners * count, dtype=jnp.int32)
        spread = (lane[None, :] // count == jnp.arange(owners, dtype=jnp.int32)[:, None]).astype(bf16)
        wanted = jnp.where(row_column(column, lane % count), row_slot(lane % count), -2).astype(f32)
        mine = jnp.dot(rank, spread, preferred_element_type=f32) == wanted
        return [
            jnp.where(mine, jnp.dot(p, spread, preferred_element_type=f32), 0.0).astype(bf16) for p in parts
        ]

    pairs = columns // 2
    pair = matrix(2 * MAIN, lambda c, r: c % 2 == r[None] // MAIN, lambda r: r[None] % MAIN)
    last = matrix(columns, lambda c, r: c == r[None], lambda r: MAIN)
    return [m.reshape(pairs, 2 * tok_rows, owners * 2 * MAIN) for m in pair] + last


def ordered(blocks):
    columns = len(blocks)
    me = lax.axis_index("expert")
    out = jnp.zeros((columns,) + blocks[0].shape, blocks[0].dtype)
    for distance, block in enumerate(blocks):
        at = ((me + distance) % columns,) + (0,) * block.ndim
        out = lax.dynamic_update_slice(out, block[None], at)
    return out


def gather_doubling(block):
    columns = lax.axis_size("expert")
    me = lax.axis_index("expert")
    have = block[None]
    distance = 1
    while distance < columns:
        other = lax.ppermute(have, "expert", [(at, at ^ distance) for at in range(columns)])
        upper = (me & distance) != 0
        have = jnp.concatenate([jnp.where(upper, other, have), jnp.where(upper, have, other)], axis=0)
        distance *= 2
    return have


def gather_ring(block):
    columns = lax.axis_size("expert")
    rise = [(at, (at + 1) % columns) for at in range(columns)]
    fall = [(at, (at - 1) % columns) for at in range(columns)]
    below, above = block, block
    blocks = {0: block}
    for distance in range(1, columns // 2):
        below = lax.ppermute(below, "expert", rise)
        above = lax.ppermute(above, "expert", fall)
        blocks[columns - distance] = below
        blocks[distance] = above
    middle = block.shape[0] // 2
    below = lax.ppermute(below[:middle], "expert", rise)
    above = lax.ppermute(above[middle:], "expert", fall)
    blocks[columns // 2] = jnp.concatenate([below, above], axis=0)
    return ordered([blocks[at] for at in range(columns)])


def per_device(tokens, router_weight, rollout_ids, source_row, gate_weight, up_weight, down_weight):
    owners = lax.axis_size("dp")
    columns = lax.axis_size("expert")
    tok_rows, model_width = tokens.shape
    top_count = rollout_ids.shape[1]
    hidden_part = gate_weight.shape[2]
    out_width = down_weight.shape[2]
    block_rows = columns * (MAIN + 1)
    slot_rows = owners * block_rows
    row_toks = columns * tok_rows
    first = FIRST_WIDTH
    second = model_width - first
    fold = -(-second // (MAIN * 128)) * 128

    raw = lax.all_gather(tokens[:, :first], "expert", axis=0, tiled=True)

    logits = jnp.dot(tokens.astype(f32), router_weight, precision=lax.Precision.HIGHEST)

    sent_ids = jnp.broadcast_to(rollout_ids.T[None], (owners, top_count, tok_rows))
    blocks = lax.all_to_all(sent_ids, "dp", split_axis=0, concat_axis=0, tiled=True)
    source_block = source_row[0] // (tok_rows * columns)
    block = lax.dynamic_index_in_dim(blocks, source_block, axis=0, keepdims=False)
    place = (source_row % tok_rows)[None, :] == jnp.arange(tok_rows, dtype=jnp.int32)[:, None]
    expert_ids = jnp.dot(
        block.astype(bf16), place.astype(bf16), preferred_element_type=f32
    ).astype(jnp.int32).T

    expert_iota = jnp.arange(router_weight.shape[1], dtype=jnp.int32)
    picks = jnp.any(expert_ids[:, :, None] == expert_iota[None, None, :], axis=1)
    chosen = picks[:, :owners]
    before = jnp.arange(tok_rows)[:, None] > jnp.arange(tok_rows)[None, :]
    slot_rank = jnp.dot(before.astype(bf16), chosen.astype(bf16), preferred_element_type=f32)
    slot_rank = jnp.where(chosen, slot_rank, -1.0)

    def select(lowest, count):
        slots = jnp.arange(lowest, lowest + count, dtype=f32)
        sel = slot_rank[:, :, None] == slots
        sel = sel.reshape(tok_rows, owners * count).astype(bf16)
        return lax.dot_general(
            sel, tokens[:, first:], (((0,), (0,)), ((), ())), preferred_element_type=f32
        ).astype(bf16)

    sent_main = select(0, MAIN).reshape(owners, MAIN, second)
    sent_last = jnp.pad(select(MAIN, 1), ((0, 0), (0, MAIN * fold - second)))
    sent_last = sent_last.reshape(owners, MAIN, fold)
    sent = jnp.concatenate([sent_main, sent_last], axis=2)
    arrived = lax.all_to_all(sent, "dp", split_axis=0, concat_axis=0, tiled=True)
    raised = jnp.where(picks, jnp.exp(jnp.where(picks, logits, 0.0)), 0.0)
    weights = raised / jnp.sum(raised, axis=1, keepdims=True)
    rank = gather_doubling(slot_rank.T.astype(bf16))
    arrived, rank, weights = lax.optimization_barrier((arrived, rank, weights))
    row_rank = jnp.transpose(rank, (1, 0, 2)).astype(f32).reshape(owners, 1, row_toks)
    tok_rank = jnp.transpose(rank, (0, 2, 1)).reshape(row_toks, owners)
    arrived_main = arrived[:, :, :second].reshape(owners * MAIN, second)
    arrived_last = arrived[:, :, second:].reshape(owners, MAIN * fold)[:, :second]
    gathered = lax.all_gather(
        jnp.concatenate([arrived_main, arrived_last], axis=0), "expert", axis=0
    )

    first_sent = first_dispatch(row_rank, raw, columns, tok_rows)
    weights, first_sent = lax.optimization_barrier((weights[:, :owners].T, first_sent))
    first_rows = lax.all_to_all(first_sent, "dp", split_axis=0, concat_axis=0, tiled=True)

    assert hidden_part % 128 == 64
    whole = hidden_part // 128 * 128
    both = jnp.concatenate(
        [part[0][:, a:b] for a, b in ((0, whole), (whole, hidden_part)) for part in (gate_weight, up_weight)],
        axis=1,
    )
    first_val = jnp.dot(
        first_rows.reshape(slot_rows, first), both[:first], preferred_element_type=f32
    ).reshape(owners, block_rows, 2 * hidden_part)
    tok_weight = jnp.transpose(gather_doubling(weights), (0, 2, 1)).reshape(row_toks, owners)
    mats = combine_matrices(tok_rank, tok_weight, columns, tok_rows)
    mats, first_val = lax.optimization_barrier((mats, first_val))

    near, far = hidden_rows(gathered, both[first:], first_val, hidden_part, CUT)
    far = lax.all_gather(far, "expert", axis=0, tiled=True)
    near = gather_ring(near).reshape(columns * hidden_part, -1)

    def project(full):
        out = lax.dot_general(full, down_weight[0], (((0,), (0,)), ((), ())), preferred_element_type=f32)
        return out.astype(bf16)

    far_main = owners * (columns - CUT) * MAIN
    near, far = project(near), project(far)
    out = jnp.concatenate(
        [
            near.reshape(owners, -1, out_width),
            far[:far_main].reshape(owners, -1, out_width),
            far[far_main:].reshape(owners, columns, out_width),
        ],
        axis=1,
    )
    back = lax.all_to_all(out, "dp", split_axis=0, concat_axis=0, tiled=True)
    part = combine(mats, back, columns).reshape(columns, tok_rows, out_width)
    whole = lax.all_to_all(part, "expert", split_axis=0, concat_axis=0, tiled=True)
    return jnp.transpose(whole, (1, 0, 2)).reshape(tok_rows, model_width)


def solution(mesh):
    in_specs = (
        P(("dp", "expert"), None),
        P(),
        P(("dp", "expert"), None),
        P(("dp", "expert")),
        P("dp", None, "expert"),
        P("dp", None, "expert"),
        P("dp", None, "expert"),
    )
    out_specs = P(("dp", "expert"), None)
    return jax.shard_map(
        per_device, mesh=mesh, in_specs=in_specs, out_specs=out_specs, check_vma=False
    )
```

profile of v0, /device:TPU:1, one launch (start us, length us, event | category | flops | bytes accessed | tf_op | source)
XLA Modules:
  0.0 363.4 jit_solution(12780296016197285586)
XLA Ops:
  6.5 1.9 slice.59
  8.5 1.3 broadcast_in_dim.96
  9.8 8.6 %all-to-all-start = ((s32[32,8,128]{2,1,0:T(8,128)}), s32[32,8,128]{2,1,0:T(8,128)S(1)}, u32[]{:S(2)}, u32[]{:S(2)}) async-start(s32[32,8,128]{2,1,0:T(8,128)} %broadcast_in_dim.96), calls=%async_computation | async-start | bytes 262144 | tf_op jit(solution)/shard_map/all_to_all | solution.py:262
  21.1 0.7 and_select_fusion.2
  21.8 4.3 %all-to-all-done = s32[32,8,128]{2,1,0:T(8,128)S(1)} async-done(((s32[32,8,128]{2,1,0:T(8,128)}), s32[32,8,128]{2,1,0:T(8,128)S(1)}, u32[]{:S(2)}, u32[]{:S(2)}) %all-to-all-start) | async-done | bytes 131104 | tf_op jit(solution)/shard_map/all_to_all | solution.py:262
  26.1 0.1 convolution_convert_fusion.3
  26.4 0.3 fusion.20
  26.6 0.1 copy.22
  26.8 0.1 convolution_select_fusion.3
  26.9 1.6 collective-permute-start
  28.5 1.3 convolution_convert_fusion.1
  29.9 0.5 fusion
  30.4 1.2 pad_maximum_fusion.4
  31.7 4.9 %all-to-all-start.1 = ((bf16[32,8,2944]{2,1,0:T(8,128)(2,1)}), bf16[32,8,2944]{2,1,0:T(8,128)(2,1)}, u32[]{:S(2)}, u32[]{:S(2)}) async-start(bf16[32,8,2944]{2,1,0:T(8,128)(2,1)} %pad_maximum_fusion.4), calls=%async_computation.1 | async-start | bytes 3014656 | tf_op jit(solution)/shard_map/all_to_all | solution.py:289
  36.7 3.1 collective-permute-start.1
  39.8 1.8 fusion.60
  41.7 5.4 %collective-permute-start.2 = (bf16[4,32,128]{2,1,0:T(8,128)(2,1)S(1)}, bf16[4,32,128]{2,1,0:T(8,128)(2,1)S(1)}, u32[]{:S(2)}, u32[]{:S(2)}) collective-permute-start(bf16[4,32,128]{2,1,0:T(8,128)(2,1)S(1)} %pad_maximum_fusion.8), channel_id=1, source_target_pairs={{0,4},{1,5},{2,6},{3,7},{4,0},{5,1},{6,2},{7,3},{8,12},{9,13},{10,... | collective-permute-start | bytes 98312 | tf_op jit(solution)/shard_map/ppermute | solution.py:218
  47.1 2.4 collective-permute-done.2
  49.5 9.2 %all-to-all-done.1 = bf16[32,8,2944]{2,1,0:T(8,128)(2,1)} async-done(((bf16[32,8,2944]{2,1,0:T(8,128)(2,1)}), bf16[32,8,2944]{2,1,0:T(8,128)(2,1)}, u32[]{:S(2)}, u32[]{:S(2)}) %all-to-all-start.1) | async-done | bytes 1507360 | tf_op jit(solution)/shard_map/all_to_all | solution.py:289
  58.7 0.9 slice.66
  59.7 1.4 slice_bitcast_fusion
  61.1 1.2 pad_maximum_fusion.5
  62.5 1.9 copy-done.3
  64.4 5.6 %shard_map.73 = bf16[32,72,1536]{2,1,0:T(8,128)(2,1)} custom-call(f32[32,1,1024]{2,1,0:T(1,128)S(1)} %bitcast.112, bf16[1024,1536]{1,0:T(8,128)(2,1)S(1)} %copy-done.3), custom_call_target="tpu_custom_call" | custom-call | tf_op jit(solution)/shard_map/pallas_call | solution.py:59
  70.0 5.2 %all-to-all-start.2 = ((bf16[32,72,1536]{2,1,0:T(8,128)(2,1)}), bf16[32,72,1536]{2,1,0:T(8,128)(2,1)}, u32[]{:S(2)}, u32[]{:S(2)}) async-start(bf16[32,72,1536]{2,1,0:T(8,128)(2,1)} %shard_map.73), calls=%async_computation.2 | async-start | bytes 14155776 | tf_op jit(solution)/shard_map/all_to_all | solution.py:304
  75.2 3.2 copy.28
  78.5 1.2 slice.76
  79.6 3.2 copy.29
  83.0 1.5 copy-done.9
  84.5 0.5 pad_maximum_fusion.1.w_ref
  85.1 0.7 collective-permute-start.3
  85.8 2.7 collective-permute-done.3
  88.5 3.3 collective-permute-start.4
  91.8 0.7 convert_compare_fusion
  92.5 2.0 collective-permute-done.4
  94.5 5.4 %collective-permute-start.5 = (f32[4,32,128]{2,1,0:T(8,128)S(1)}, f32[4,32,128]{2,1,0:T(8,128)S(1)}, u32[]{:S(2)}, u32[]{:S(2)}) collective-permute-start(f32[4,32,128]{2,1,0:T(8,128)S(1)} %pad_maximum_fusion.7), channel_id=1, source_target_pairs={{0,4},{1,5},{2,6},{3,7},{4,0},{5,1},{6,2},{7,3},{8,12},{9,13},{10,... | collective-permute-start | bytes 196616 | tf_op jit(solution)/shard_map/ppermute | solution.py:218
  99.9 0.4 convolution_compare_fusion
  100.3 3.1 collective-permute-done.5
  103.4 1.1 fusion.8.last_low
  104.6 1.2 fusion.7.last_high
  105.7 0.5 select_convert_fusion
  106.2 1.4 select_convert_fusion.1
  107.6 55.4 %all-to-all-done.2 = bf16[32,72,1536]{2,1,0:T(8,128)(2,1)} async-done(((bf16[32,72,1536]{2,1,0:T(8,128)(2,1)}), bf16[32,72,1536]{2,1,0:T(8,128)(2,1)}, u32[]{:S(2)}, u32[]{:S(2)}) %all-to-all-start.2) | async-done | bytes 7077920 | tf_op jit(solution)/shard_map/all_to_all | solution.py:304
  163.0 9.2 %fusion.9.v_ref = f32[32,72,384]{2,1,0:T(8,128)} fusion(bf16[32,72,1536]{2,1,0:T(8,128)(2,1)} %all-to-all-done.2, bf16[4096,64]{1,0:T(8,128)(2,1)} %copy-done.11, bf16[4096,64]{1,0:T(8,128)(2,1)} %slice.76, bf16[4096,128]{1,0:T(8,128)(2,1)} %copy-done.10, bf16[4096,128]{1,0:T(8,128)(2,1)} %copy-done.8), kind=kOutput, calls=%fused_computation.24 | convolution fusion | flops 2722627584 | bytes 13762560 | tf_op jit(solution)/shard_map/dot_general | solution.py:312
  172.2 17.3 %all-gather.9.cloned.1.call-done = bf16[2304,2560]{1,0:T(8,128)(2,1)} async-done(((bf16[288,2560]{1,0:T(8,128)(2,1)}), bf16[2304,2560]{1,0:T(8,128)(2,1)}) %all-gather.9.cloned.1.call-update) | async-done | bytes 11796496 | tf_op jit(solution)/shard_map/all_gather | solution.py:298
  189.5 11.0 %shard_map.74 = (bf16[192,1024]{1,0:T(8,128)(2,1)S(1)}, bf16[192,1280]{1,0:T(8,128)(2,1)S(1)}) custom-call(bf16[8,288,2560]{2,1,0:T(8,128)(2,1)} %bitcast.113, bf16[2560,384]{1,0:T(8,128)(2,1)S(1)} %pad_maximum_fusion.1.w_ref, f32[32,72,384]{2,1,0:T(8,128)} %fusion.9.v_ref), custom_call_target="tpu_custom_call" | custom-call | tf_op jit(solution)/shard_map/pallas_call | solution.py:136
  200.5 0.8 copy-done.6
  201.4 2.2 collective-permute-start.6
  203.6 7.8 %collective-permute-done.6 = bf16[192,1024]{1,0:T(8,128)(2,1)S(1)} collective-permute-done((bf16[192,1024]{1,0:T(8,128)(2,1)S(1)}, bf16[192,1024]{1,0:T(8,128)(2,1)S(1)}, u32[]{:S(2)}, u32[]{:S(2)}) %collective-permute-start.6) | collective-permute-done | bytes 393248 | tf_op jit(solution)/shard_map/ppermute | solution.py:233
  211.4 3.4 collective-permute-start.7
  214.7 0.4 broadcast_in_dim.107
  215.2 16.1 %collective-permute-done.7 = bf16[192,1024]{1,0:T(8,128)(2,1)S(1)} collective-permute-done((bf16[192,1024]{1,0:T(8,128)(2,1)S(1)}, bf16[192,1024]{1,0:T(8,128)(2,1)S(1)}, u32[]{:S(2)}, u32[]{:S(2)}) %collective-permute-start.7) | collective-permute-done | bytes 393248 | tf_op jit(solution)/shard_map/ppermute | solution.py:233
  231.3 3.5 collective-permute-start.8
  234.9 19.7 %collective-permute-done.11 = bf16[192,1024]{1,0:T(8,128)(2,1)S(1)} collective-permute-done((bf16[192,1024]{1,0:T(8,128)(2,1)S(1)}, bf16[192,1024]{1,0:T(8,128)(2,1)S(1)}, u32[]{:S(2)}, u32[]{:S(2)}) %collective-permute-start.11) | collective-permute-done | bytes 393248 | tf_op jit(solution)/shard_map/ppermute | solution.py:232
  254.8 2.7 collective-permute-start.13
  257.5 8.3 %collective-permute-done.12 = bf16[96,1024]{1,0:T(8,128)(2,1)S(1)} collective-permute-done((bf16[96,1024]{1,0:T(8,128)(2,1)S(1)}, bf16[96,1024]{1,0:T(8,128)(2,1)S(1)}, u32[]{:S(2)}, u32[]{:S(2)}) %collective-permute-start.12) | collective-permute-done | bytes 196640 | tf_op jit(solution)/shard_map/ppermute | solution.py:237
  266.0 1.8 fusion.4
  267.9 7.3 %all-gather.7.cloned.1.call-done = bf16[1536,1280]{1,0:T(8,128)(2,1)} async-done(((bf16[192,1280]{1,0:T(8,128)(2,1)}), bf16[1536,1280]{1,0:T(8,128)(2,1)}) %all-gather.7.cloned.1.call-update) | async-done | bytes 3932176 | tf_op jit(solution)/shard_map/all_gather | solution.py:320
  275.2 4.8 %convolution_convert_fusion.2 = bf16[1280,512]{1,0:T(8,128)(2,1)S(1)} fusion(bf16[1536,1280]{1,0:T(8,128)(2,1)} %all-gather.7.cloned.1.call-done, bf16[1,1536,512]{2,1,0:T(8,128)(2,1)} %param.13), kind=kOutput, calls=%fused_computation.3 | convolution fusion | flops 2013921280 | bytes 6815744 | tf_op jit(solution)/shard_map/dot_general | solution.py:324
  280.1 0.2 pad_maximum_fusion
  280.4 39.0 %all_to_all.25.back_ref = bf16[32,72,512]{2,1,0:T(8,128)(2,1)} all-to-all(bf16[32,72,512]{2,1,0:T(8,128)(2,1)S(1)} %pad_maximum_fusion), channel_id=1, replica_groups=mesh['dp'=32,'expert'=8] {'dp'}, dimensions={0} | all-to-all | bytes 4718592 | tf_op jit(solution)/shard_map/all_to_all | solution.py:337
  319.4 3.6 shard_map.75
  323.0 32.8 %all_to_all.26 = bf16[8,128,512]{2,1,0:T(8,128)(2,1)S(1)} all-to-all(bf16[8,128,512]{2,1,0:T(8,128)(2,1)S(1)} %bitcast.111), channel_id=1, replica_groups=mesh['dp'=32,'expert'=8] {'expert'}, dimensions={0} | all-to-all | bytes 2097152 | tf_op jit(solution)/shard_map/all_to_all | solution.py:339
  355.8 1.1 copy.33
  (83 shorter events, 1.4 us)
Async XLA Ops:
  6.5 33.3 %copy-start = (f32[4096,128]{1,0:T(8,128)S(1)}, f32[4096,128]{1,0:T(8,128)}, u32[]{:S(2)}) copy-start(f32[4096,128]{1,0:T(8,128)} %param.8) | copy-start | bytes 6291460
  6.5 23.4 %copy-start.7 = (bf16[128,4096]{1,0:T(8,128)(2,1)S(1)}, bf16[128,4096]{1,0:T(8,128)(2,1)}, u32[]{:S(2)}) copy-start(bf16[128,4096]{1,0:T(8,128)(2,1)} %param.7) | copy-start | bytes 3145732
  6.5 56.0 %all-gather.5.cloned.1.call-start = ((), (), s32[]{:S(2)}) async-start(), calls=%async_computation.5 | async-start | bytes 3538944 | tf_op jit(solution)/shard_map/all_gather | solution.py:257
  9.8 16.3 %all-to-all-start = ((s32[32,8,128]{2,1,0:T(8,128)}), s32[32,8,128]{2,1,0:T(8,128)S(1)}, u32[]{:S(2)}, u32[]{:S(2)}) async-start(s32[32,8,128]{2,1,0:T(8,128)} %broadcast_in_dim.96), calls=%async_computation | async-start | bytes 262144 | tf_op jit(solution)/shard_map/all_to_all | solution.py:262
  26.9 9.8 %collective-permute-start = (bf16[1,32,128]{2,1,0:T(8,128)(2,1)S(1)}, bf16[1,32,128]{2,1,0:T(8,128)(2,1)S(1)}, u32[]{:S(2)}, u32[]{:S(2)}) collective-permute-start(bf16[1,32,128]{2,1,0:T(8,128)(2,1)S(1)} %convert_bitcast_fusion.1), channel_id=1, source_target_pairs={{0,1},{1,0},{2,3},{3,2},{4,5},{5,4},{6,7},{7,6},{8,9},{9,8},{10,11... | collective-permute-start | bytes 24584 | tf_op jit(solution)/shard_map/ppermute | solution.py:218
  31.7 27.0 %all-to-all-start.1 = ((bf16[32,8,2944]{2,1,0:T(8,128)(2,1)}), bf16[32,8,2944]{2,1,0:T(8,128)(2,1)}, u32[]{:S(2)}, u32[]{:S(2)}) async-start(bf16[32,8,2944]{2,1,0:T(8,128)(2,1)} %pad_maximum_fusion.4), calls=%async_computation.1 | async-start | bytes 3014656 | tf_op jit(solution)/shard_map/all_to_all | solution.py:289
  36.6 152.9 %all-gather.9.cloned.1.call-start = ((), (), s32[]{:S(2)}) async-start(), calls=%async_computation.7 | async-start | bytes 13271040 | tf_op jit(solution)/shard_map/all_gather | solution.py:298
  36.7 4.9 %collective-permute-start.1 = (bf16[2,32,128]{2,1,0:T(8,128)(2,1)S(1)}, bf16[2,32,128]{2,1,0:T(8,128)(2,1)S(1)}, u32[]{:S(2)}, u32[]{:S(2)}) collective-permute-start(bf16[2,32,128]{2,1,0:T(8,128)(2,1)S(1)} %pad_maximum_fusion.10), channel_id=1, source_target_pairs={{0,2},{1,3},{2,0},{3,1},{4,6},{5,7},{6,4},{7,5},{8,10},{9,11},{10,... | collective-permute-start | bytes 49160 | tf_op jit(solution)/shard_map/ppermute | solution.py:218
  41.7 7.8 %collective-permute-start.2 = (bf16[4,32,128]{2,1,0:T(8,128)(2,1)S(1)}, bf16[4,32,128]{2,1,0:T(8,128)(2,1)S(1)}, u32[]{:S(2)}, u32[]{:S(2)}) collective-permute-start(bf16[4,32,128]{2,1,0:T(8,128)(2,1)S(1)} %pad_maximum_fusion.8), channel_id=1, source_target_pairs={{0,4},{1,5},{2,6},{3,7},{4,0},{5,1},{6,2},{7,3},{8,12},{9,13},{10,... | collective-permute-start | bytes 98312 | tf_op jit(solution)/shard_map/ppermute | solution.py:218
  62.5 1.9 copy-start.3
  70.0 93.0 %all-to-all-start.2 = ((bf16[32,72,1536]{2,1,0:T(8,128)(2,1)}), bf16[32,72,1536]{2,1,0:T(8,128)(2,1)}, u32[]{:S(2)}, u32[]{:S(2)}) async-start(bf16[32,72,1536]{2,1,0:T(8,128)(2,1)} %shard_map.73), calls=%async_computation.2 | async-start | bytes 14155776 | tf_op jit(solution)/shard_map/all_to_all | solution.py:304
  75.2 200.0 %all-gather.7.cloned.1.call-start = ((), (), s32[]{:S(2)}) async-start(), calls=%async_computation.6 | async-start | bytes 4423680 | tf_op jit(solution)/shard_map/all_gather | solution.py:320
  78.5 6.6 %copy-start.8 = (bf16[4096,128]{1,0:T(8,128)(2,1)}, bf16[4096,128]{1,0:T(8,128)(2,1)S(1)}, u32[]{:S(2)}) copy-start(bf16[4096,128]{1,0:T(8,128)(2,1)S(1)} %slice.74) | copy-start | bytes 3145732
  82.8 1.7 copy-start.9
  82.9 2.2 copy-start.10
  83.0 2.1 copy-start.11
  85.1 3.4 collective-permute-start.3
  88.5 6.0 %collective-permute-start.4 = (f32[2,32,128]{2,1,0:T(8,128)S(1)}, f32[2,32,128]{2,1,0:T(8,128)S(1)}, u32[]{:S(2)}, u32[]{:S(2)}) collective-permute-start(f32[2,32,128]{2,1,0:T(8,128)S(1)} %pad_maximum_fusion.9), channel_id=1, source_target_pairs={{0,2},{1,3},{2,0},{3,1},{4,6},{5,7},{6,4},{7,5},{8,10},{9,11},{10,... | collective-permute-start | bytes 98312 | tf_op jit(solution)/shard_map/ppermute | solution.py:218
  94.5 8.9 %collective-permute-start.5 = (f32[4,32,128]{2,1,0:T(8,128)S(1)}, f32[4,32,128]{2,1,0:T(8,128)S(1)}, u32[]{:S(2)}, u32[]{:S(2)}) collective-permute-start(f32[4,32,128]{2,1,0:T(8,128)S(1)} %pad_maximum_fusion.7), channel_id=1, source_target_pairs={{0,4},{1,5},{2,6},{3,7},{4,0},{5,1},{6,2},{7,3},{8,12},{9,13},{10,... | collective-permute-start | bytes 196616 | tf_op jit(solution)/shard_map/ppermute | solution.py:218
  200.5 0.8 copy-start.6
  201.4 10.0 %collective-permute-start.6 = (bf16[192,1024]{1,0:T(8,128)(2,1)S(1)}, bf16[192,1024]{1,0:T(8,128)(2,1)S(1)}, u32[]{:S(2)}, u32[]{:S(2)}) collective-permute-start(bf16[192,1024]{1,0:T(8,128)(2,1)S(1)} %get-tuple-element.27), channel_id=1, source_target_pairs={{0,7},{1,0},{2,1},{3,2},{4,3},{5,4},{6,5},{7,6},{8,15},{9,8},{10,9... | collective-permute-start | bytes 1179656 | tf_op jit(solution)/shard_map/ppermute | solution.py:233
  203.6 11.1 %collective-permute-start.9 = (bf16[192,1024]{1,0:T(8,128)(2,1)S(1)}, bf16[192,1024]{1,0:T(8,128)(2,1)S(1)}, u32[]{:S(2)}, u32[]{:S(2)}) collective-permute-start(bf16[192,1024]{1,0:T(8,128)(2,1)S(1)} %get-tuple-element.27), channel_id=1, source_target_pairs={{0,1},{1,2},{2,3},{3,4},{4,5},{5,6},{6,7},{7,0},{8,9},{9,10},{10,1... | collective-permute-start | bytes 1179656 | tf_op jit(solution)/shard_map/ppermute | solution.py:232
  211.4 19.9 %collective-permute-start.7 = (bf16[192,1024]{1,0:T(8,128)(2,1)S(1)}, bf16[192,1024]{1,0:T(8,128)(2,1)S(1)}, u32[]{:S(2)}, u32[]{:S(2)}) collective-permute-start(bf16[192,1024]{1,0:T(8,128)(2,1)S(1)} %collective-permute-done.6), channel_id=1, source_target_pairs={{0,7},{1,0},{2,1},{3,2},{4,3},{5,4},{6,5},{7,6},{8,15},{9,8},{10,9... | collective-permute-start | bytes 1179656 | tf_op jit(solution)/shard_map/ppermute | solution.py:233
  214.7 20.1 %collective-permute-start.10 = (bf16[192,1024]{1,0:T(8,128)(2,1)S(1)}, bf16[192,1024]{1,0:T(8,128)(2,1)S(1)}, u32[]{:S(2)}, u32[]{:S(2)}) collective-permute-start(bf16[192,1024]{1,0:T(8,128)(2,1)S(1)} %collective-permute-done.9), channel_id=1, source_target_pairs={{0,1},{1,2},{2,3},{3,4},{4,5},{5,6},{6,7},{7,0},{8,9},{9,10},{10,1... | collective-permute-start | bytes 1179656 | tf_op jit(solution)/shard_map/ppermute | solution.py:232
  231.3 23.4 %collective-permute-start.8 = (bf16[192,1024]{1,0:T(8,128)(2,1)S(1)}, bf16[192,1024]{1,0:T(8,128)(2,1)S(1)}, u32[]{:S(2)}, u32[]{:S(2)}) collective-permute-start(bf16[192,1024]{1,0:T(8,128)(2,1)S(1)} %collective-permute-done.7), channel_id=1, source_target_pairs={{0,7},{1,0},{2,1},{3,2},{4,3},{5,4},{6,5},{7,6},{8,15},{9,8},{10,9... | collective-permute-start | bytes 1179656 | tf_op jit(solution)/shard_map/ppermute | solution.py:233
  234.8 19.8 %collective-permute-start.11 = (bf16[192,1024]{1,0:T(8,128)(2,1)S(1)}, bf16[192,1024]{1,0:T(8,128)(2,1)S(1)}, u32[]{:S(2)}, u32[]{:S(2)}) collective-permute-start(bf16[192,1024]{1,0:T(8,128)(2,1)S(1)} %collective-permute-done.10), channel_id=1, source_target_pairs={{0,1},{1,2},{2,3},{3,4},{4,5},{5,6},{6,7},{7,0},{8,9},{9,10},{10,1... | collective-permute-start | bytes 1179656 | tf_op jit(solution)/shard_map/ppermute | solution.py:232
  234.9 31.1 %copy-start.12 = (bf16[1,1536,512]{2,1,0:T(8,128)(2,1)S(1)}, bf16[1,1536,512]{2,1,0:T(8,128)(2,1)}, u32[]{:S(2)}) copy-start(bf16[1,1536,512]{2,1,0:T(8,128)(2,1)} %param.13) | copy-start | bytes 4718596
  254.6 11.2 %collective-permute-start.12 = (bf16[96,1024]{1,0:T(8,128)(2,1)S(1)}, bf16[96,1024]{1,0:T(8,128)(2,1)S(1)}, u32[]{:S(2)}, u32[]{:S(2)}) collective-permute-start(bf16[96,1024]{1,0:T(8,128)(2,1)S(1)} %slice.79), channel_id=1, source_target_pairs={{0,1},{1,2},{2,3},{3,4},{4,5},{5,6},{6,7},{7,0},{8,9},{9,10},{10,1... | collective-permute-start | bytes 589832 | tf_op jit(solution)/shard_map/ppermute | solution.py:237
  254.8 11.1 %collective-permute-start.13 = (bf16[96,1024]{1,0:T(8,128)(2,1)S(1)}, bf16[96,1024]{1,0:T(8,128)(2,1)S(1)}, u32[]{:S(2)}, u32[]{:S(2)}) collective-permute-start(bf16[96,1024]{1,0:T(8,128)(2,1)S(1)} %slice.80), channel_id=1, source_target_pairs={{0,7},{1,0},{2,1},{3,2},{4,3},{5,4},{6,5},{7,6},{8,15},{9,8},{10,9... | collective-permute-start | bytes 589832 | tf_op jit(solution)/shard_map/ppermute | solution.py:238
  280.3 39.1 %copy-start.2 = (bf16[1024,512]{1,0:T(8,128)(2,1)S(1)}, bf16[1024,512]{1,0:T(8,128)(2,1)}, u32[]{:S(2)}) copy-start(bf16[1024,512]{1,0:T(8,128)(2,1)} %select_convert_fusion.1) | copy-start | bytes 3145732
  280.4 39.1 %copy-start.4 = (bf16[1024,256]{1,0:T(8,128)(2,1)S(1)}, bf16[1024,256]{1,0:T(8,128)(2,1)}, u32[]{:S(2)}) copy-start(bf16[1024,256]{1,0:T(8,128)(2,1)} %fusion.8.last_low) | copy-start | bytes 1572868
  280.4 39.0 %copy-start.5 = (bf16[1024,256]{1,0:T(8,128)(2,1)S(1)}, bf16[1024,256]{1,0:T(8,128)(2,1)}, u32[]{:S(2)}) copy-start(bf16[1024,256]{1,0:T(8,128)(2,1)} %fusion.7.last_high) | copy-start | bytes 1572868
  319.4 37.5 %copy-start.1 = (f32[4096,128]{1,0:T(8,128)S(1)}, f32[4096,128]{1,0:T(8,128)}, u32[]{:S(2)}) copy-start(f32[4096,128]{1,0:T(8,128)} %param.8) | copy-start | bytes 6291460
Sparse Core Ops, SparseCore 0:
  9.1 50.0 all-gather.4
  62.5 126.9 all-gather.8
  201.5 73.6 all-gather.6
where the time goes:
time: 364 us; the launch traced here: 363 us
  waiting for transfers between devices  156 us (43%)
  blocking collectives  71.8 us (20%)
  starting transfers between devices  50.2 us (14%)
  matrix products  25 us (7%)
  Pallas kernels  20.2 us (6%)
  local copies, waits for them, and re-layouts  19.9 us (5%)
  between operations  16.3 us (4%)
  other arithmetic  4.28 us (1%)
    all_to_all x1, waiting for transfers between devices, per_device(): lax.all_to_all(first_sent, 'dp', split_axis=0, concat_axis=0, tiled=True)  55.4 us
    all_to_all x1, blocking collectives, per_device(): back = lax.all_to_all(out, 'dp', split_axis=0, concat_axis=0, tiled=True)  39 us
    all_to_all x1, blocking collectives, per_device(): lax.all_to_all(part, 'expert', split_axis=0, concat_axis=0, tiled=True)  32.8 us
    ppermute x3, waiting for transfers between devices, gather_ring(): above = lax.ppermute(above, 'expert', fall)  23.9 us
    ppermute x3, waiting for transfers between devices, gather_ring(): below = lax.ppermute(below, 'expert', rise)  19.7 us
    ppermute x6, starting transfers between devices, gather_doubling(): lax.ppermute(have, 'expert', [(at, at ^ distance) for at in range(columns)])  19.5 us
    all_gather x1, waiting for transfers between devices, per_device(): lax.all_gather(jnp.concatenate([arrived_main, arrived_last], axis=0), 'ex...  17.3 us
    pallas_call x1, Pallas kernels, hidden_rows(): pl.pallas_call(functools.partial(hidden_kernel, owners, cut), grid=(steps...  11 us
  transfers between devices with their start and end apart: 20, of which 13 were waited for; matrix products, arithmetic and copies ran while one was open for 10% of the time, Pallas kernels for 2%

commit v1 on v0

--- a/solution.py
+++ b/solution.py
@@ -11,7 +11,7 @@
 FIRST_WIDTH = 1536
 HIDDEN_STEPS = 3
 CUT = 4
-DISPATCH_STEPS = 1
+DISPATCH_STEPS = 2
 VMEM_BYTES = 48 * 1024 * 1024
 bf16, f32 = jnp.bfloat16, jnp.float32
 

time: 364 us -> 364 us (level)
  transfers between devices with their start and end apart: 20 -> 20, of which waited for: 13 -> 13; matrix products, arithmetic and copies ran while one was open for 10% -> 10% of each run, Pallas kernels for 2% -> 1%
where the time goes in v1:
time: 364 us; the launch traced here: 363 us
  waiting for transfers between devices  156 us (43%)
  blocking collectives  71.9 us (20%)
  starting transfers between devices  50.2 us (14%)
  matrix products  25 us (7%)
  local copies, waits for them, and re-layouts  19.9 us (5%)
  Pallas kernels  19.8 us (5%)
  between operations  16.3 us (4%)
  other arithmetic  4.28 us (1%)
    all_to_all x1, waiting for transfers between devices, per_device(): lax.all_to_all(first_sent, 'dp', split_axis=0, concat_axis=0, tiled=True)  55.3 us
    all_to_all x1, blocking collectives, per_device(): back = lax.all_to_all(out, 'dp', split_axis=0, concat_axis=0, tiled=True)  39 us
    all_to_all x1, blocking collectives, per_device(): lax.all_to_all(part, 'expert', split_axis=0, concat_axis=0, tiled=True)  32.9 us
    ppermute x3, waiting for transfers between devices, gather_ring(): above = lax.ppermute(above, 'expert', fall)  23.9 us
    ppermute x3, waiting for transfers between devices, gather_ring(): below = lax.ppermute(below, 'expert', rise)  19.8 us
    ppermute x6, starting transfers between devices, gather_doubling(): lax.ppermute(have, 'expert', [(at, at ^ distance) for at in range(columns)])  19.5 us
    all_gather x1, waiting for transfers between devices, per_device(): lax.all_gather(jnp.concatenate([arrived_main, arrived_last], axis=0), 'ex...  17.6 us
    pallas_call x1, Pallas kernels, hidden_rows(): pl.pallas_call(functools.partial(hidden_kernel, owners, cut), grid=(steps...  11 us
  transfers between devices with their start and end apart: 20, of which 13 were waited for; matrix products, arithmetic and copies ran while one was open for 10% of the time, Pallas kernels for 1%

profile of v1, /device:TPU:1, one launch (start us, length us, event | category | flops | bytes accessed | tf_op | source)
XLA Modules:
  0.0 363.2 jit_solution(6387229817522414702)
XLA Ops:
  6.5 1.9 slice.59
  8.5 1.3 broadcast_in_dim.96
  9.8 8.6 %all-to-all-start = ((s32[32,8,128]{2,1,0:T(8,128)}), s32[32,8,128]{2,1,0:T(8,128)S(1)}, u32[]{:S(2)}, u32[]{:S(2)}) async-start(s32[32,8,128]{2,1,0:T(8,128)} %broadcast_in_dim.96), calls=%async_computation | async-start | bytes 262144 | tf_op jit(solution)/shard_map/all_to_all | solution.py:262
  21.1 0.7 and_select_fusion.2
  21.8 4.3 %all-to-all-done = s32[32,8,128]{2,1,0:T(8,128)S(1)} async-done(((s32[32,8,128]{2,1,0:T(8,128)}), s32[32,8,128]{2,1,0:T(8,128)S(1)}, u32[]{:S(2)}, u32[]{:S(2)}) %all-to-all-start) | async-done | bytes 131104 | tf_op jit(solution)/shard_map/all_to_all | solution.py:262
  26.1 0.1 convolution_convert_fusion.3
  26.4 0.3 fusion.20
  26.6 0.1 copy.22
  26.8 0.1 convolution_select_fusion.3
  26.9 1.6 collective-permute-start
  28.5 1.3 convolution_convert_fusion.1
  29.9 0.5 fusion
  30.4 1.2 pad_maximum_fusion.4
  31.7 4.9 %all-to-all-start.1 = ((bf16[32,8,2944]{2,1,0:T(8,128)(2,1)}), bf16[32,8,2944]{2,1,0:T(8,128)(2,1)}, u32[]{:S(2)}, u32[]{:S(2)}) async-start(bf16[32,8,2944]{2,1,0:T(8,128)(2,1)} %pad_maximum_fusion.4), calls=%async_computation.1 | async-start | bytes 3014656 | tf_op jit(solution)/shard_map/all_to_all | solution.py:289
  36.7 3.1 collective-permute-start.1
  39.8 1.8 fusion.60
  41.7 5.4 %collective-permute-start.2 = (bf16[4,32,128]{2,1,0:T(8,128)(2,1)S(1)}, bf16[4,32,128]{2,1,0:T(8,128)(2,1)S(1)}, u32[]{:S(2)}, u32[]{:S(2)}) collective-permute-start(bf16[4,32,128]{2,1,0:T(8,128)(2,1)S(1)} %pad_maximum_fusion.8), channel_id=1, source_target_pairs={{0,4},{1,5},{2,6},{3,7},{4,0},{5,1},{6,2},{7,3},{8,12},{9,13},{10,... | collective-permute-start | bytes 98312 | tf_op jit(solution)/shard_map/ppermute | solution.py:218
  47.1 2.4 collective-permute-done.2
  49.5 9.2 %all-to-all-done.1 = bf16[32,8,2944]{2,1,0:T(8,128)(2,1)} async-done(((bf16[32,8,2944]{2,1,0:T(8,128)(2,1)}), bf16[32,8,2944]{2,1,0:T(8,128)(2,1)}, u32[]{:S(2)}, u32[]{:S(2)}) %all-to-all-start.1) | async-done | bytes 1507360 | tf_op jit(solution)/shard_map/all_to_all | solution.py:289
  58.7 0.9 slice.66
  59.7 1.4 slice_bitcast_fusion
  61.1 1.2 pad_maximum_fusion.5
  62.5 1.9 copy-done.3
  64.4 5.2 %shard_map.73 = bf16[32,72,1536]{2,1,0:T(8,128)(2,1)} custom-call(f32[32,1,1024]{2,1,0:T(1,128)S(1)} %bitcast.112, bf16[1024,1536]{1,0:T(8,128)(2,1)S(1)} %copy-done.3), custom_call_target="tpu_custom_call" | custom-call | tf_op jit(solution)/shard_map/pallas_call | solution.py:59
  69.6 5.2 %all-to-all-start.2 = ((bf16[32,72,1536]{2,1,0:T(8,128)(2,1)}), bf16[32,72,1536]{2,1,0:T(8,128)(2,1)}, u32[]{:S(2)}, u32[]{:S(2)}) async-start(bf16[32,72,1536]{2,1,0:T(8,128)(2,1)} %shard_map.73), calls=%async_computation.2 | async-start | bytes 14155776 | tf_op jit(solution)/shard_map/all_to_all | solution.py:304
  74.9 3.2 copy.28
  78.1 1.2 slice.76
  79.3 3.2 copy.29
  82.7 1.5 copy-done.9
  84.2 0.5 pad_maximum_fusion.1.w_ref
  84.8 0.7 collective-permute-start.3
  85.4 2.7 collective-permute-done.3
  88.2 3.1 collective-permute-start.4
  91.3 0.7 convert_compare_fusion
  92.0 2.1 collective-permute-done.4
  94.1 5.6 %collective-permute-start.5 = (f32[4,32,128]{2,1,0:T(8,128)S(1)}, f32[4,32,128]{2,1,0:T(8,128)S(1)}, u32[]{:S(2)}, u32[]{:S(2)}) collective-permute-start(f32[4,32,128]{2,1,0:T(8,128)S(1)} %pad_maximum_fusion.7), channel_id=1, source_target_pairs={{0,4},{1,5},{2,6},{3,7},{4,0},{5,1},{6,2},{7,3},{8,12},{9,13},{10,... | collective-permute-start | bytes 196616 | tf_op jit(solution)/shard_map/ppermute | solution.py:218
  99.6 0.4 convolution_compare_fusion
  100.0 3.1 collective-permute-done.5
  103.2 1.1 fusion.8.last_low
  104.3 1.2 fusion.7.last_high
  105.5 0.5 select_convert_fusion
  105.9 1.4 select_convert_fusion.1
  107.3 55.3 %all-to-all-done.2 = bf16[32,72,1536]{2,1,0:T(8,128)(2,1)} async-done(((bf16[32,72,1536]{2,1,0:T(8,128)(2,1)}), bf16[32,72,1536]{2,1,0:T(8,128)(2,1)}, u32[]{:S(2)}, u32[]{:S(2)}) %all-to-all-start.2) | async-done | bytes 7077920 | tf_op jit(solution)/shard_map/all_to_all | solution.py:304
  162.7 9.2 %fusion.9.v_ref = f32[32,72,384]{2,1,0:T(8,128)} fusion(bf16[32,72,1536]{2,1,0:T(8,128)(2,1)} %all-to-all-done.2, bf16[4096,64]{1,0:T(8,128)(2,1)} %copy-done.11, bf16[4096,64]{1,0:T(8,128)(2,1)} %slice.76, bf16[4096,128]{1,0:T(8,128)(2,1)} %copy-done.10, bf16[4096,128]{1,0:T(8,128)(2,1)} %copy-done.8), kind=kOutput, calls=%fused_computation.24 | convolution fusion | flops 2722627584 | bytes 13762560 | tf_op jit(solution)/shard_map/dot_general | solution.py:312
  171.9 17.6 %all-gather.9.cloned.1.call-done = bf16[2304,2560]{1,0:T(8,128)(2,1)} async-done(((bf16[288,2560]{1,0:T(8,128)(2,1)}), bf16[2304,2560]{1,0:T(8,128)(2,1)}) %all-gather.9.cloned.1.call-update) | async-done | bytes 11796496 | tf_op jit(solution)/shard_map/all_gather | solution.py:298
  189.5 11.0 %shard_map.74 = (bf16[192,1024]{1,0:T(8,128)(2,1)S(1)}, bf16[192,1280]{1,0:T(8,128)(2,1)S(1)}) custom-call(bf16[8,288,2560]{2,1,0:T(8,128)(2,1)} %bitcast.113, bf16[2560,384]{1,0:T(8,128)(2,1)S(1)} %pad_maximum_fusion.1.w_ref, f32[32,72,384]{2,1,0:T(8,128)} %fusion.9.v_ref), custom_call_target="tpu_custom_call" | custom-call | tf_op jit(solution)/shard_map/pallas_call | solution.py:136
  200.5 0.8 copy-done.6
  201.4 2.2 collective-permute-start.6
  203.6 7.8 %collective-permute-done.6 = bf16[192,1024]{1,0:T(8,128)(2,1)S(1)} collective-permute-done((bf16[192,1024]{1,0:T(8,128)(2,1)S(1)}, bf16[192,1024]{1,0:T(8,128)(2,1)S(1)}, u32[]{:S(2)}, u32[]{:S(2)}) %collective-permute-start.6) | collective-permute-done | bytes 393248 | tf_op jit(solution)/shard_map/ppermute | solution.py:233
  211.4 3.4 collective-permute-start.7
  214.7 0.4 broadcast_in_dim.107
  215.2 16.1 %collective-permute-done.7 = bf16[192,1024]{1,0:T(8,128)(2,1)S(1)} collective-permute-done((bf16[192,1024]{1,0:T(8,128)(2,1)S(1)}, bf16[192,1024]{1,0:T(8,128)(2,1)S(1)}, u32[]{:S(2)}, u32[]{:S(2)}) %collective-permute-start.7) | collective-permute-done | bytes 393248 | tf_op jit(solution)/shard_map/ppermute | solution.py:233
  231.3 3.5 collective-permute-start.8
  234.9 19.7 %collective-permute-done.11 = bf16[192,1024]{1,0:T(8,128)(2,1)S(1)} collective-permute-done((bf16[192,1024]{1,0:T(8,128)(2,1)S(1)}, bf16[192,1024]{1,0:T(8,128)(2,1)S(1)}, u32[]{:S(2)}, u32[]{:S(2)}) %collective-permute-start.11) | collective-permute-done | bytes 393248 | tf_op jit(solution)/shard_map/ppermute | solution.py:232
  254.8 2.7 collective-permute-start.13
  257.5 8.3 %collective-permute-done.12 = bf16[96,1024]{1,0:T(8,128)(2,1)S(1)} collective-permute-done((bf16[96,1024]{1,0:T(8,128)(2,1)S(1)}, bf16[96,1024]{1,0:T(8,128)(2,1)S(1)}, u32[]{:S(2)}, u32[]{:S(2)}) %collective-permute-start.12) | collective-permute-done | bytes 196640 | tf_op jit(solution)/shard_map/ppermute | solution.py:237
  266.1 1.8 fusion.4
  267.9 6.9 %all-gather.7.cloned.1.call-done = bf16[1536,1280]{1,0:T(8,128)(2,1)} async-done(((bf16[192,1280]{1,0:T(8,128)(2,1)}), bf16[1536,1280]{1,0:T(8,128)(2,1)}) %all-gather.7.cloned.1.call-update) | async-done | bytes 3932176 | tf_op jit(solution)/shard_map/all_gather | solution.py:320
  274.9 4.8 %convolution_convert_fusion.2 = bf16[1280,512]{1,0:T(8,128)(2,1)S(1)} fusion(bf16[1536,1280]{1,0:T(8,128)(2,1)} %all-gather.7.cloned.1.call-done, bf16[1,1536,512]{2,1,0:T(8,128)(2,1)} %param.13), kind=kOutput, calls=%fused_computation.3 | convolution fusion | flops 2013921280 | bytes 6815744 | tf_op jit(solution)/shard_map/dot_general | solution.py:324
  279.8 0.2 pad_maximum_fusion
  280.0 39.0 %all_to_all.25.back_ref = bf16[32,72,512]{2,1,0:T(8,128)(2,1)} all-to-all(bf16[32,72,512]{2,1,0:T(8,128)(2,1)S(1)} %pad_maximum_fusion), channel_id=1, replica_groups=mesh['dp'=32,'expert'=8] {'dp'}, dimensions={0} | all-to-all | bytes 4718592 | tf_op jit(solution)/shard_map/all_to_all | solution.py:337
  319.1 3.6 shard_map.75
  322.7 32.9 %all_to_all.26 = bf16[8,128,512]{2,1,0:T(8,128)(2,1)S(1)} all-to-all(bf16[8,128,512]{2,1,0:T(8,128)(2,1)S(1)} %bitcast.111), channel_id=1, replica_groups=mesh['dp'=32,'expert'=8] {'expert'}, dimensions={0} | all-to-all | bytes 2097152 | tf_op jit(solution)/shard_map/all_to_all | solution.py:339
  355.6 1.1 copy.33
  (83 shorter events, 1.5 us)
Async XLA Ops:
  6.5 33.3 %copy-start = (f32[4096,128]{1,0:T(8,128)S(1)}, f32[4096,128]{1,0:T(8,128)}, u32[]{:S(2)}) copy-start(f32[4096,128]{1,0:T(8,128)} %param.8) | copy-start | bytes 6291460
  6.5 23.4 %copy-start.7 = (bf16[128,4096]{1,0:T(8,128)(2,1)S(1)}, bf16[128,4096]{1,0:T(8,128)(2,1)}, u32[]{:S(2)}) copy-start(bf16[128,4096]{1,0:T(8,128)(2,1)} %param.7) | copy-start | bytes 3145732
  6.5 56.0 %all-gather.5.cloned.1.call-start = ((), (), s32[]{:S(2)}) async-start(), calls=%async_computation.5 | async-start | bytes 3538944 | tf_op jit(solution)/shard_map/all_gather | solution.py:257
  9.8 16.3 %all-to-all-start = ((s32[32,8,128]{2,1,0:T(8,128)}), s32[32,8,128]{2,1,0:T(8,128)S(1)}, u32[]{:S(2)}, u32[]{:S(2)}) async-start(s32[32,8,128]{2,1,0:T(8,128)} %broadcast_in_dim.96), calls=%async_computation | async-start | bytes 262144 | tf_op jit(solution)/shard_map/all_to_all | solution.py:262
  26.9 9.8 %collective-permute-start = (bf16[1,32,128]{2,1,0:T(8,128)(2,1)S(1)}, bf16[1,32,128]{2,1,0:T(8,128)(2,1)S(1)}, u32[]{:S(2)}, u32[]{:S(2)}) collective-permute-start(bf16[1,32,128]{2,1,0:T(8,128)(2,1)S(1)} %convert_bitcast_fusion.1), channel_id=1, source_target_pairs={{0,1},{1,0},{2,3},{3,2},{4,5},{5,4},{6,7},{7,6},{8,9},{9,8},{10,11... | collective-permute-start | bytes 24584 | tf_op jit(solution)/shard_map/ppermute | solution.py:218
  31.7 27.0 %all-to-all-start.1 = ((bf16[32,8,2944]{2,1,0:T(8,128)(2,1)}), bf16[32,8,2944]{2,1,0:T(8,128)(2,1)}, u32[]{:S(2)}, u32[]{:S(2)}) async-start(bf16[32,8,2944]{2,1,0:T(8,128)(2,1)} %pad_maximum_fusion.4), calls=%async_computation.1 | async-start | bytes 3014656 | tf_op jit(solution)/shard_map/all_to_all | solution.py:289
  36.6 152.9 %all-gather.9.cloned.1.call-start = ((), (), s32[]{:S(2)}) async-start(), calls=%async_computation.7 | async-start | bytes 13271040 | tf_op jit(solution)/shard_map/all_gather | solution.py:298
  36.7 4.9 %collective-permute-start.1 = (bf16[2,32,128]{2,1,0:T(8,128)(2,1)S(1)}, bf16[2,32,128]{2,1,0:T(8,128)(2,1)S(1)}, u32[]{:S(2)}, u32[]{:S(2)}) collective-permute-start(bf16[2,32,128]{2,1,0:T(8,128)(2,1)S(1)} %pad_maximum_fusion.10), channel_id=1, source_target_pairs={{0,2},{1,3},{2,0},{3,1},{4,6},{5,7},{6,4},{7,5},{8,10},{9,11},{10,... | collective-permute-start | bytes 49160 | tf_op jit(solution)/shard_map/ppermute | solution.py:218
  41.7 7.8 %collective-permute-start.2 = (bf16[4,32,128]{2,1,0:T(8,128)(2,1)S(1)}, bf16[4,32,128]{2,1,0:T(8,128)(2,1)S(1)}, u32[]{:S(2)}, u32[]{:S(2)}) collective-permute-start(bf16[4,32,128]{2,1,0:T(8,128)(2,1)S(1)} %pad_maximum_fusion.8), channel_id=1, source_target_pairs={{0,4},{1,5},{2,6},{3,7},{4,0},{5,1},{6,2},{7,3},{8,12},{9,13},{10,... | collective-permute-start | bytes 98312 | tf_op jit(solution)/shard_map/ppermute | solution.py:218
  62.5 1.9 copy-start.3
  69.6 93.0 %all-to-all-start.2 = ((bf16[32,72,1536]{2,1,0:T(8,128)(2,1)}), bf16[32,72,1536]{2,1,0:T(8,128)(2,1)}, u32[]{:S(2)}, u32[]{:S(2)}) async-start(bf16[32,72,1536]{2,1,0:T(8,128)(2,1)} %shard_map.73), calls=%async_computation.2 | async-start | bytes 14155776 | tf_op jit(solution)/shard_map/all_to_all | solution.py:304
  74.8 200.0 %all-gather.7.cloned.1.call-start = ((), (), s32[]{:S(2)}) async-start(), calls=%async_computation.6 | async-start | bytes 4423680 | tf_op jit(solution)/shard_map/all_gather | solution.py:320
  78.1 6.6 %copy-start.8 = (bf16[4096,128]{1,0:T(8,128)(2,1)}, bf16[4096,128]{1,0:T(8,128)(2,1)S(1)}, u32[]{:S(2)}) copy-start(bf16[4096,128]{1,0:T(8,128)(2,1)S(1)} %slice.74) | copy-start | bytes 3145732
  82.5 1.7 copy-start.9
  82.5 2.2 copy-start.10
  82.6 2.1 copy-start.11
  84.8 3.4 collective-permute-start.3
  88.2 5.9 %collective-permute-start.4 = (f32[2,32,128]{2,1,0:T(8,128)S(1)}, f32[2,32,128]{2,1,0:T(8,128)S(1)}, u32[]{:S(2)}, u32[]{:S(2)}) collective-permute-start(f32[2,32,128]{2,1,0:T(8,128)S(1)} %pad_maximum_fusion.9), channel_id=1, source_target_pairs={{0,2},{1,3},{2,0},{3,1},{4,6},{5,7},{6,4},{7,5},{8,10},{9,11},{10,... | collective-permute-start | bytes 98312 | tf_op jit(solution)/shard_map/ppermute | solution.py:218
  94.1 9.1 %collective-permute-start.5 = (f32[4,32,128]{2,1,0:T(8,128)S(1)}, f32[4,32,128]{2,1,0:T(8,128)S(1)}, u32[]{:S(2)}, u32[]{:S(2)}) collective-permute-start(f32[4,32,128]{2,1,0:T(8,128)S(1)} %pad_maximum_fusion.7), channel_id=1, source_target_pairs={{0,4},{1,5},{2,6},{3,7},{4,0},{5,1},{6,2},{7,3},{8,12},{9,13},{10,... | collective-permute-start | bytes 196616 | tf_op jit(solution)/shard_map/ppermute | solution.py:218
  200.5 0.8 copy-start.6
  201.4 10.0 %collective-permute-start.6 = (bf16[192,1024]{1,0:T(8,128)(2,1)S(1)}, bf16[192,1024]{1,0:T(8,128)(2,1)S(1)}, u32[]{:S(2)}, u32[]{:S(2)}) collective-permute-start(bf16[192,1024]{1,0:T(8,128)(2,1)S(1)} %get-tuple-element.27), channel_id=1, source_target_pairs={{0,7},{1,0},{2,1},{3,2},{4,3},{5,4},{6,5},{7,6},{8,15},{9,8},{10,9... | collective-permute-start | bytes 1179656 | tf_op jit(solution)/shard_map/ppermute | solution.py:233
  203.6 11.1 %collective-permute-start.9 = (bf16[192,1024]{1,0:T(8,128)(2,1)S(1)}, bf16[192,1024]{1,0:T(8,128)(2,1)S(1)}, u32[]{:S(2)}, u32[]{:S(2)}) collective-permute-start(bf16[192,1024]{1,0:T(8,128)(2,1)S(1)} %get-tuple-element.27), channel_id=1, source_target_pairs={{0,1},{1,2},{2,3},{3,4},{4,5},{5,6},{6,7},{7,0},{8,9},{9,10},{10,1... | collective-permute-start | bytes 1179656 | tf_op jit(solution)/shard_map/ppermute | solution.py:232
  211.4 19.9 %collective-permute-start.7 = (bf16[192,1024]{1,0:T(8,128)(2,1)S(1)}, bf16[192,1024]{1,0:T(8,128)(2,1)S(1)}, u32[]{:S(2)}, u32[]{:S(2)}) collective-permute-start(bf16[192,1024]{1,0:T(8,128)(2,1)S(1)} %collective-permute-done.6), channel_id=1, source_target_pairs={{0,7},{1,0},{2,1},{3,2},{4,3},{5,4},{6,5},{7,6},{8,15},{9,8},{10,9... | collective-permute-start | bytes 1179656 | tf_op jit(solution)/shard_map/ppermute | solution.py:233
  214.7 20.1 %collective-permute-start.10 = (bf16[192,1024]{1,0:T(8,128)(2,1)S(1)}, bf16[192,1024]{1,0:T(8,128)(2,1)S(1)}, u32[]{:S(2)}, u32[]{:S(2)}) collective-permute-start(bf16[192,1024]{1,0:T(8,128)(2,1)S(1)} %collective-permute-done.9), channel_id=1, source_target_pairs={{0,1},{1,2},{2,3},{3,4},{4,5},{5,6},{6,7},{7,0},{8,9},{9,10},{10,1... | collective-permute-start | bytes 1179656 | tf_op jit(solution)/shard_map/ppermute | solution.py:232
  231.3 23.5 %collective-permute-start.8 = (bf16[192,1024]{1,0:T(8,128)(2,1)S(1)}, bf16[192,1024]{1,0:T(8,128)(2,1)S(1)}, u32[]{:S(2)}, u32[]{:S(2)}) collective-permute-start(bf16[192,1024]{1,0:T(8,128)(2,1)S(1)} %collective-permute-done.7), channel_id=1, source_target_pairs={{0,7},{1,0},{2,1},{3,2},{4,3},{5,4},{6,5},{7,6},{8,15},{9,8},{10,9... | collective-permute-start | bytes 1179656 | tf_op jit(solution)/shard_map/ppermute | solution.py:233
  234.8 19.8 %collective-permute-start.11 = (bf16[192,1024]{1,0:T(8,128)(2,1)S(1)}, bf16[192,1024]{1,0:T(8,128)(2,1)S(1)}, u32[]{:S(2)}, u32[]{:S(2)}) collective-permute-start(bf16[192,1024]{1,0:T(8,128)(2,1)S(1)} %collective-permute-done.10), channel_id=1, source_target_pairs={{0,1},{1,2},{2,3},{3,4},{4,5},{5,6},{6,7},{7,0},{8,9},{9,10},{10,1... | collective-permute-start | bytes 1179656 | tf_op jit(solution)/shard_map/ppermute | solution.py:232
  234.9 31.2 %copy-start.12 = (bf16[1,1536,512]{2,1,0:T(8,128)(2,1)S(1)}, bf16[1,1536,512]{2,1,0:T(8,128)(2,1)}, u32[]{:S(2)}) copy-start(bf16[1,1536,512]{2,1,0:T(8,128)(2,1)} %param.13) | copy-start | bytes 4718596
  254.6 11.2 %collective-permute-start.12 = (bf16[96,1024]{1,0:T(8,128)(2,1)S(1)}, bf16[96,1024]{1,0:T(8,128)(2,1)S(1)}, u32[]{:S(2)}, u32[]{:S(2)}) collective-permute-start(bf16[96,1024]{1,0:T(8,128)(2,1)S(1)} %slice.79), channel_id=1, source_target_pairs={{0,1},{1,2},{2,3},{3,4},{4,5},{5,6},{6,7},{7,0},{8,9},{9,10},{10,1... | collective-permute-start | bytes 589832 | tf_op jit(solution)/shard_map/ppermute | solution.py:237
  254.8 11.1 %collective-permute-start.13 = (bf16[96,1024]{1,0:T(8,128)(2,1)S(1)}, bf16[96,1024]{1,0:T(8,128)(2,1)S(1)}, u32[]{:S(2)}, u32[]{:S(2)}) collective-permute-start(bf16[96,1024]{1,0:T(8,128)(2,1)S(1)} %slice.80), channel_id=1, source_target_pairs={{0,7},{1,0},{2,1},{3,2},{4,3},{5,4},{6,5},{7,6},{8,15},{9,8},{10,9... | collective-permute-start | bytes 589832 | tf_op jit(solution)/shard_map/ppermute | solution.py:238
  280.0 39.1 %copy-start.2 = (bf16[1024,512]{1,0:T(8,128)(2,1)S(1)}, bf16[1024,512]{1,0:T(8,128)(2,1)}, u32[]{:S(2)}) copy-start(bf16[1024,512]{1,0:T(8,128)(2,1)} %select_convert_fusion.1) | copy-start | bytes 3145732
  280.0 39.1 %copy-start.4 = (bf16[1024,256]{1,0:T(8,128)(2,1)S(1)}, bf16[1024,256]{1,0:T(8,128)(2,1)}, u32[]{:S(2)}) copy-start(bf16[1024,256]{1,0:T(8,128)(2,1)} %fusion.8.last_low) | copy-start | bytes 1572868
  280.0 39.0 %copy-start.5 = (bf16[1024,256]{1,0:T(8,128)(2,1)S(1)}, bf16[1024,256]{1,0:T(8,128)(2,1)}, u32[]{:S(2)}) copy-start(bf16[1024,256]{1,0:T(8,128)(2,1)} %fusion.7.last_high) | copy-start | bytes 1572868
  319.1 37.6 %copy-start.1 = (f32[4096,128]{1,0:T(8,128)S(1)}, f32[4096,128]{1,0:T(8,128)}, u32[]{:S(2)}) copy-start(f32[4096,128]{1,0:T(8,128)} %param.8) | copy-start | bytes 6291460
Sparse Core Ops, SparseCore 0:
  9.1 50.0 all-gather.4
  62.5 126.9 all-gather.8
  201.5 73.3 all-gather.6
